TPU v7x, 256 devices: a whole 4x4x8 slice. The times are simulated.
256 devices in a mesh: gx: 32 (over y, z_lo, core), gy: 8 (over z_hi, x).
Axes of the slice: x: 4, y: 4, z: 8 (z_hi: 2, z_lo: 4; z = z_hi * 4 + z_lo), core: 2. Of those that a mesh axis runs over, the one named last changes fastest.
Arguments:
- control: bfloat16 [2048, 8, 2048], P('gx', None, 'gy'), may hold values from -6 to 6
- innovation: float32 [2048, 8, 2048], P('gx', None, 'gy'), may hold values from -6 to 6
- obs_weight: float32 [2048, 8, 2048], P('gx', None, 'gy'), may hold values from 0.5 to 4
- courant_x: float32 [2048, 8, 2048], P('gx', None, 'gy'), may hold values from -0.9 to 0.9
- courant_y: float32 [2048, 8, 2048], P('gx', None, 'gy'), may hold values from -0.9 to 0.9
- filter_x: bfloat16 [2048, 2048], P('gx'), may hold values from -3 to 3
- filter_y: bfloat16 [2048, 2048], P('gy'), may hold values from -3 to 3
Outputs:
- end_state: float32 [2048, 8, 2048], P('gx', None, 'gy')
- gradient: float32 [2048, 8, 2048], P('gx', None, 'gy')
All inputs are finite; a program needn't handle non-finite values.
Results may differ from a plain program's by a relative error of at most 0.0029.
Values may be sent and summed in bfloat16 or wider, within the bound.
A program may use at most 128 MiB of HBM per device.

v0:
```python
import jax
import jax.numpy as jnp
from jax import lax
from jax.sharding import PartitionSpec as P


def extended(array, sides, width):
    for axis, dim in sides:
        size, length = (lax.axis_size(axis), array.shape[dim])
        up = [(i, (i + 1) % size) for i in range(size - 1)]
        down = [(j, i) for i, j in up]
        last = lax.slice_in_dim(array, length - width, length, axis=dim)
        initial = lax.slice_in_dim(array, 0, width, axis=dim)
        before = lax.ppermute(last, axis, up)
        after = lax.ppermute(initial, axis, down)
        array = jnp.concatenate([before, array, after], axis=dim)
    return array


def per_device(control, innovation, obs_weight, courant_x, courant_y, filter_x, filter_y):
    columns = filter_x
    smoothed = jnp.einsum(
        "ij,jlc->ilc",
        columns,
        lax.all_gather(control, "gx", axis=0, tiled=True),
        preferred_element_type=jnp.float32,
    ).astype(jnp.bfloat16)
    columns = filter_y
    start_state = jnp.einsum(
        "kc,xlc->xlk",
        columns,
        lax.all_gather(smoothed, "gy", axis=2, tiled=True),
        preferred_element_type=jnp.float32,
    )
    padded = extended(start_state, (("gx", 0), ("gy", 2)), 1)
    end_state = (
        start_state
        - courant_x * (padded[2:, :, 1:-1] - padded[:-2, :, 1:-1]) * 0.5
        - courant_y * (padded[1:-1, :, 2:] - padded[1:-1, :, :-2]) * 0.5
    )
    misfit = obs_weight * (end_state - innovation)
    fluxes = jnp.stack([courant_x * misfit, courant_y * misfit])
    rim_cells = extended(fluxes, (("gx", 1), ("gy", 3)), 1)
    adjoint = (
        misfit
        + 0.5 * (rim_cells[0, 2:, :, 1:-1] - rim_cells[0, :-2, :, 1:-1])
        + 0.5 * (rim_cells[1, 1:-1, :, 2:] - rim_cells[1, 1:-1, :, :-2])
    ).astype(jnp.bfloat16)
    partial_sums = jnp.einsum("kc,xlk->xlc", filter_y, adjoint, preferred_element_type=jnp.float32)
    pulled = lax.psum_scatter(partial_sums, "gy", scatter_dimension=2, tiled=True).astype(
        jnp.bfloat16
    )
    columns = filter_x
    carried = lax.psum_scatter(
        jnp.einsum("ij,ilc->jlc", columns, pulled, preferred_element_type=jnp.float32),
        "gx",
        scatter_dimension=0,
        tiled=True,
    )
    gradient = control.astype(jnp.float32) + carried
    return (end_state, gradient)


def solution(mesh):
    placed = (
        P("gx", None, "gy"),
        P("gx", None, "gy"),
        P("gx", None, "gy"),
        P("gx", None, "gy"),
        P("gx", None, "gy"),
        P("gx", None),
        P("gy", None),
    )
    return jax.shard_map(
        per_device,
        mesh=mesh,
        in_specs=placed,
        out_specs=(P("gx", None, "gy"), P("gx", None, "gy")),
        check_vma=False,
    )
```

profile of v0, /device:TPU:2, one launch (start us, length us, event | category | flops | bytes accessed | tf_op | source)
XLA Modules:
  0.0 578.3 jit_solution(11222078684383102453)
XLA Ops:
  7.2 0.0 copy-start
  7.2 0.0 all-gather.3.cloned.1.call-start
  7.2 0.7 all-gather.3.cloned.1.call-update
  7.9 0.0 all-gather.5.cloned.1.call-start
  8.0 74.1 %all-gather.3.cloned.1.call-done = bf16[2048,8,256]{2,1,0:T(8,128)(2,1)} async-done(((bf16[64,8,256]{2,1,0:T(8,128)(2,1)}), bf16[2048,8,256]{2,1,0:T(8,128)(2,1)}) %all-gather.3.cloned.1.call-update) | async-done | bytes 8388624 | tf_op jit(solution)/shard_map/all_gather | solution.py:25
  82.0 5.1 fusion
  87.1 0.9 copy.24
  88.0 0.0 all-gather.5.cloned.1.call-update
  88.0 0.0 copy-start.1
  88.0 0.0 copy-start.3
  88.0 0.0 reduce-scatter.3.cloned.1.call-start
  88.1 75.3 %all-gather.5.cloned.1.call-done = bf16[64,8,2048]{2,1,0:T(8,128)(2,1)} async-done(((bf16[64,8,256]{2,1,0:T(8,128)(2,1)}), bf16[64,8,2048]{2,1,0:T(8,128)(2,1)}) %all-gather.5.cloned.1.call-update) | async-done | bytes 2097168 | tf_op jit(solution)/shard_map/all_gather | solution.py:32
  163.4 2.3 fusion.4
  165.7 1.3 collective-permute-start.1
  167.0 1.3 collective-permute-start
  168.3 0.0 collective-permute-done.1
  168.4 2.7 collective-permute-done
  171.1 0.1 fusion.29
  171.2 2.8 collective-permute-start.2
  174.0 3.1 collective-permute-start.3
  177.0 3.9 collective-permute-done.2
  180.9 3.1 collective-permute-done.3
  184.0 2.4 multiply_bitcast_fusion.1
  186.5 0.1 multiply_bitcast_fusion
  186.6 2.9 collective-permute-start.5
  189.5 1.3 collective-permute-start.4
  190.8 0.0 collective-permute-done.5
  190.8 3.1 collective-permute-done.4
  193.9 0.1 pad_maximum_fusion
  193.9 1.0 fusion.28
  194.9 1.3 copy.11
  196.2 1.9 collective-permute-start.6
  198.1 0.3 copy.13
  198.4 3.9 collective-permute-start.7
  202.3 0.0 collective-permute-done.6
  202.3 0.3 copy.12
  202.7 1.3 collective-permute-done.7
  203.9 1.1 copy.14
  205.0 1.4 fusion.10
  206.4 2.7 fusion.2
  209.1 0.0 reduce-scatter.3.cloned.1.call-update
  209.1 0.0 reduce-scatter.5.cloned.1.call-start
  209.1 145.5 %reduce-scatter.3.cloned.1.call-done = f32[64,8,256]{2,0,1:T(8,128)} async-done(((f32[64,8,2048]{2,0,1:T(8,128)}), f32[64,8,256]{2,0,1:T(8,128)}) %reduce-scatter.3.cloned.1.call-update) | async-done | bytes 524304 | tf_op jit(solution)/shard_map/reduce_scatter | solution.py:50
  354.6 9.1 %convolution_bitcast_fusion = f32[2048,8,256]{0,2,1:T(8,128)} fusion(bf16[64,2048]{1,0:T(8,128)(2,1)S(1)} %copy-done.4, f32[64,8,256]{2,0,1:T(8,128)} %reduce-scatter.3.cloned.1.call-done), kind=kOutput, calls=%fused_computation.2 | convolution fusion | flops 537001984 | bytes 17563648 | tf_op jit(solution)/shard_map/ij,ilc->jlc/dot_general | solution.py:55
  363.8 17.8 %copy.15 = f32[2048,8,256]{2,1,0:T(8,128)} copy(f32[2048,8,256]{0,2,1:T(8,128)} %convolution_bitcast_fusion) | data formatting | bytes 33554432 | tf_op jit(solution)/shard_map/ij,ilc->jlc/dot_general | solution.py:55
  381.6 0.0 reduce-scatter.5.cloned.1.call-update
  381.6 188.3 %reduce-scatter.5.cloned.1.call-done = f32[64,8,256]{2,1,0:T(8,128)} async-done(((f32[2048,8,256]{2,1,0:T(8,128)}), f32[64,8,256]{2,1,0:T(8,128)}) %reduce-scatter.5.cloned.1.call-update) | async-done | bytes 524304 | tf_op jit(solution)/shard_map/reduce_scatter | solution.py:54
  569.9 1.9 convert_add_fusion
  (10 shorter events, 0.1 us)
Async XLA Ops:
  7.2 156.2 %copy-start = (bf16[256,2048]{1,0:T(8,128)(2,1)S(1)}, bf16[256,2048]{1,0:T(8,128)(2,1)}, u32[]{:S(2)}) copy-start(bf16[256,2048]{1,0:T(8,128)(2,1)} %param.13) | copy-start | bytes 3145732
  7.2 74.9 %all-gather.3.cloned.1.call-start = ((), (), s32[]{:S(2)}) async-start(), calls=%async_computation.2 | async-start | bytes 8650752 | tf_op jit(solution)/shard_map/all_gather | solution.py:25
  7.9 155.5 %all-gather.5.cloned.1.call-start = ((), (), s32[]{:S(2)}) async-start(), calls=%async_computation.3 | async-start | bytes 2359296 | tf_op jit(solution)/shard_map/all_gather | solution.py:32
  88.0 96.0 %copy-start.1 = (f32[64,8,256]{2,1,0:T(8,128)S(1)}, f32[64,8,256]{2,1,0:T(8,128)}, u32[]{:S(2)}) copy-start(f32[64,8,256]{2,1,0:T(8,128)} %param.11) | copy-start | bytes 1572868
  88.0 96.0 %copy-start.3 = (f32[64,8,256]{2,1,0:T(8,128)S(1)}, f32[64,8,256]{2,1,0:T(8,128)}, u32[]{:S(2)}) copy-start(f32[64,8,256]{2,1,0:T(8,128)} %param.10) | copy-start | bytes 1572868
  88.0 266.6 %reduce-scatter.3.cloned.1.call-start = ((), (), s32[]{:S(2)}) async-start(), calls=%async_computation.4 | async-start | bytes 4718592 | tf_op jit(solution)/shard_map/reduce_scatter | solution.py:50
  165.7 2.6 collective-permute-start.1
  167.0 4.0 collective-permute-start
  171.2 9.8 %collective-permute-start.2 = (f32[66,8,1]{2,1,0:T(8,128)S(1)}, f32[66,8,1]{2,1,0:T(8,128)S(1)}, u32[]{:S(2)}, u32[]{:S(2)}) collective-permute-start(f32[66,8,1]{2,1,0:T(8,128)S(1)} %get-tuple-element.11), channel_id=1, source_target_pairs={{1,0},{2,1},{3,2},{4,3},{5,4},{6,5},{7,6},{9,8},{10,9},{11,10},{12... | collective-permute-start | bytes 6344 | tf_op jit(solution)/shard_map/ppermute | solution.py:15
  174.0 10.1 %collective-permute-start.3 = (f32[66,8,1]{2,1,0:T(8,128)S(1)}, f32[66,8,1]{2,1,0:T(8,128)S(1)}, u32[]{:S(2)}, u32[]{:S(2)}) collective-permute-start(f32[66,8,1]{2,1,0:T(8,128)S(1)} %get-tuple-element.12), channel_id=1, source_target_pairs={{0,1},{1,2},{2,3},{3,4},{4,5},{5,6},{6,7},{8,9},{9,10},{10,11},{11... | collective-permute-start | bytes 6344 | tf_op jit(solution)/shard_map/ppermute | solution.py:14
  186.6 4.2 collective-permute-start.5
  189.5 4.4 collective-permute-start.4
  196.2 6.1 %collective-permute-start.6 = (f32[2,66,8,1]{1,2,3,0:T(8,128)S(1)}, f32[2,66,8,1]{1,2,3,0:T(8,128)S(1)}, u32[]{:S(2)}, u32[]{:S(2)}) collective-permute-start(f32[2,66,8,1]{1,2,3,0:T(8,128)S(1)} %copy.11), channel_id=1, source_target_pairs={{1,0},{2,1},{3,2},{4,3},{5,4},{6,5},{7,6},{9,8},{10,9},{11,10},{12... | collective-permute-start | bytes 12680 | tf_op jit(solution)/shard_map/ppermute | solution.py:15
  198.4 5.5 collective-permute-start.7
  209.1 145.6 %copy-start.4 = (bf16[64,2048]{1,0:T(8,128)(2,1)S(1)}, bf16[64,2048]{1,0:T(8,128)(2,1)}, u32[]{:S(2)}) copy-start(bf16[64,2048]{1,0:T(8,128)(2,1)} %param.12) | copy-start | bytes 786436
  209.1 360.8 %reduce-scatter.5.cloned.1.call-start = ((), (), s32[]{:S(2)}) async-start(), calls=%async_computation.5 | async-start | bytes 17301504 | tf_op jit(solution)/shard_map/reduce_scatter | solution.py:54
  381.6 188.3 %copy-start.2 = (bf16[64,8,256]{2,1,0:T(8,128)(2,1)S(1)}, bf16[64,8,256]{2,1,0:T(8,128)(2,1)}, u32[]{:S(2)}) copy-start(bf16[64,8,256]{2,1,0:T(8,128)(2,1)} %param.7) | copy-start | bytes 786436
Sparse Core Ops, SparseCore 0:
  9.9 72.1 all-gather.2
  88.1 75.2 all-gather.4
  209.2 145.3 reduce-scatter.2
  381.7 188.1 reduce-scatter.4
where the time goes:
time: 579 us; the launch traced here: 578 us
  waiting for transfers between devices  498 us (86%)
  local copies, waits for them, and re-layouts  22.8 us (4%)
  matrix products  19.2 us (3%)
  starting transfers between devices  18.6 us (3%)
  between operations  13.9 us (2%)
  other arithmetic  5.88 us (1%)
    reduce_scatter x1, waiting for transfers between devices, per_device(): lax.psum_scatter(jnp.einsum('ij,ilc->jlc', columns, pulled, preferred_ele...  188 us
    reduce_scatter x1, waiting for transfers between devices, per_device(): lax.psum_scatter(partial_sums, 'gy', scatter_dimension=2, tiled=True)  145 us
    all_gather x1, waiting for transfers between devices, per_device(): lax.all_gather(smoothed, 'gy', axis=2, tiled=True)  75.3 us
    all_gather x1, waiting for transfers between devices, per_device(): lax.all_gather(control, 'gx', axis=0, tiled=True)  74.1 us
    dot_general x1, local copies, waits for them, and re-layouts, per_device(): jnp.einsum('ij,ilc->jlc', columns, pulled, preferred_element_type=jnp.flo...  17.8 us
  transfers between devices with their start and end apart: 12, of which 9 were waited for; matrix products, arithmetic and copies ran while one was open for 0% of the time, Pallas kernels for 0%

commit v1 on v0

--- a/solution.py
+++ b/solution.py
@@ -2,6 +2,13 @@
 import jax.numpy as jnp
 from jax import lax
 from jax.sharding import PartitionSpec as P
+
+
+def _settle_zone(here_x, across):
+    moved = tuple((here_x for _ in range(jax.lax.axis_size(across))))
+    arr_now = jnp.stack(moved)
+    view_out = jax.lax.all_to_all(arr_now, across, 0, 0)
+    return jnp.concatenate(view_out, axis=2)
 
 
 def extended(array, sides, width):
@@ -27,10 +34,7 @@
     ).astype(jnp.bfloat16)
     columns = filter_y
     start_state = jnp.einsum(
-        "kc,xlc->xlk",
-        columns,
-        lax.all_gather(smoothed, "gy", axis=2, tiled=True),
-        preferred_element_type=jnp.float32,
+        "kc,xlc->xlk", columns, _settle_zone(smoothed, "gy"), preferred_element_type=jnp.float32
     )
     padded = extended(start_state, (("gx", 0), ("gy", 2)), 1)
     end_state = (

time: 579 us -> 559 us (0.965)
  waiting for transfers between devices: 498 us -> 421 us
  blocking collectives: 0 us -> 58.3 us
    all_gather x1 -> x0, waiting for transfers between devices: 75.3 us -> none  [per_device(): lax.all_gather(smoothed, 'gy', axis=2, tiled=True)]
    all_to_all x0 -> x1, blocking collectives: none -> 58.3 us  [_settle_zone(): view_out = jax.lax.all_to_all(arr_now, across, 0, 0)]
  transfers between devices with their start and end apart: 12 -> 11, of which waited for: 9 -> 8; matrix products, arithmetic and copies ran while one was open for 0% -> 0% of each run, Pallas kernels for 0% -> 0%
where the time goes in v1:
time: 559 us
  waiting for transfers between devices  421 us (75%)
  blocking collectives  58.3 us (10%)
  local copies, waits for them, and re-layouts  24.3 us (4%)
  starting transfers between devices  18.6 us (3%)
  matrix products  17.6 us (3%)
  between operations  14 us (3%)
    reduce_scatter x1, waiting for transfers between devices, per_device(): lax.psum_scatter(jnp.einsum('ij,ilc->jlc', columns, pulled, preferred_ele...  188 us
    reduce_scatter x1, waiting for transfers between devices, per_device(): lax.psum_scatter(partial_sums, 'gy', scatter_dimension=2, tiled=True)  142 us
    all_gather x1, waiting for transfers between devices, per_device(): lax.all_gather(control, 'gx', axis=0, tiled=True)  73.7 us
    all_to_all x1, blocking collectives, _settle_zone(): view_out = jax.lax.all_to_all(arr_now, across, 0, 0)  58.3 us
    dot_general x1, local copies, waits for them, and re-layouts, per_device(): jnp.einsum('ij,ilc->jlc', columns, pulled, preferred_element_type=jnp.flo...  17.8 us
    ppermute x4, waiting for transfers between devices, extended(): after = lax.ppermute(initial, axis, down)  12.2 us
  transfers between devices with their start and end apart: 11, of which 8 were waited for; matrix products, arithmetic and copies ran while one was open for 0% of the time, Pallas kernels for 0%

profile of v1, /device:TPU:2, one launch (start us, length us, event | category | flops | bytes accessed | tf_op | source)
XLA Modules:
  0.0 558.7 jit_solution(6831188639178378537)
XLA Ops:
  7.2 0.0 copy-start
  7.2 0.0 all-gather.2.cloned.1.call-start
  7.2 1.8 copy.13
  9.0 0.0 all-gather.2.cloned.1.call-update
  9.0 0.0 reduce-scatter.3.cloned.1.call-start
  9.1 73.7 %all-gather.2.cloned.1.call-done = bf16[2048,8,256]{2,0,1:T(8,128)(2,1)} async-done(((bf16[64,8,256]{2,0,1:T(8,128)(2,1)}), bf16[2048,8,256]{2,0,1:T(8,128)(2,1)}) %all-gather.2.cloned.1.call-update) | async-done | bytes 8388624 | tf_op jit(solution)/shard_map/all_gather | solution.py:32
  82.8 5.0 convolution_convert_fusion
  87.8 0.2 copy.14
  88.0 0.1 stack.8
  88.1 58.3 %all_to_all.5 = bf16[8,64,8,256]{3,2,1,0:T(8,128)(2,1)S(1)} all-to-all(bf16[8,64,8,256]{3,2,1,0:T(8,128)(2,1)S(1)} %stack.8), channel_id=1, replica_groups=mesh['gx'=32,'gy'=8] {'gy'}, dimensions={0} | all-to-all | bytes 4194304 | tf_op jit(solution)/shard_map/all_to_all | solution.py:10
  146.5 0.3 copy.15
  146.7 0.0 copy-start.1
  146.8 0.0 copy-start.4
  146.8 0.0 copy-start.5
  146.8 0.0 copy-start.6
  146.8 0.8 fusion.2
  147.6 1.3 collective-permute-start.1
  148.9 1.3 collective-permute-start
  150.2 4.8 collective-permute-done
  155.0 0.1 fusion.27
  155.2 3.6 collective-permute-start.2
  158.8 2.2 collective-permute-start.3
  161.0 3.9 collective-permute-done.2
  164.9 4.0 collective-permute-done.3
  168.9 1.2 multiply_bitcast_fusion.1
  170.1 0.1 multiply_bitcast_fusion
  170.2 2.9 collective-permute-start.5
  173.1 1.3 collective-permute-start.4
  174.4 3.5 collective-permute-done.4
  178.0 0.1 pad_maximum_fusion
  178.1 1.0 fusion.26
  179.0 1.3 copy.16
  180.3 1.9 collective-permute-start.6
  182.3 0.3 copy.18
  182.5 3.9 collective-permute-start.7
  186.5 0.3 copy.17
  186.8 1.3 collective-permute-done.7
  188.1 1.1 copy.19
  189.2 1.4 fusion.8
  190.5 2.6 fusion
  193.2 0.0 reduce-scatter.3.cloned.1.call-update
  193.2 0.0 reduce-scatter.5.cloned.1.call-start
  193.3 141.8 %reduce-scatter.3.cloned.1.call-done = f32[64,8,256]{2,0,1:T(8,128)} async-done(((f32[64,8,2048]{2,0,1:T(8,128)}), f32[64,8,256]{2,0,1:T(8,128)}) %reduce-scatter.3.cloned.1.call-update) | async-done | bytes 524304 | tf_op jit(solution)/shard_map/reduce_scatter | solution.py:54
  335.0 9.1 %convolution_bitcast_fusion = f32[2048,8,256]{0,2,1:T(8,128)} fusion(bf16[64,2048]{1,0:T(8,128)(2,1)S(1)} %copy-done.2, f32[64,8,256]{2,0,1:T(8,128)} %reduce-scatter.3.cloned.1.call-done), kind=kOutput, calls=%fused_computation | convolution fusion | flops 537001984 | bytes 17563648 | tf_op jit(solution)/shard_map/ij,ilc->jlc/dot_general | solution.py:59
  344.2 17.8 %copy.20 = f32[2048,8,256]{2,1,0:T(8,128)} copy(f32[2048,8,256]{0,2,1:T(8,128)} %convolution_bitcast_fusion) | data formatting | bytes 33554432 | tf_op jit(solution)/shard_map/ij,ilc->jlc/dot_general | solution.py:59
  362.0 0.0 reduce-scatter.5.cloned.1.call-update
  362.0 188.3 %reduce-scatter.5.cloned.1.call-done = f32[64,8,256]{2,1,0:T(8,128)} async-done(((f32[2048,8,256]{2,1,0:T(8,128)}), f32[64,8,256]{2,1,0:T(8,128)}) %reduce-scatter.5.cloned.1.call-update) | async-done | bytes 524304 | tf_op jit(solution)/shard_map/reduce_scatter | solution.py:58
  550.3 1.9 convert_add_fusion
  (15 shorter events, 0.1 us)
Async XLA Ops:
  7.2 139.6 %copy-start = (bf16[256,2048]{1,0:T(8,128)(2,1)S(1)}, bf16[256,2048]{1,0:T(8,128)(2,1)}, u32[]{:S(2)}) copy-start(bf16[256,2048]{1,0:T(8,128)(2,1)} %param.13) | copy-start | bytes 3145732
  7.2 75.6 %all-gather.2.cloned.1.call-start = ((), (), s32[]{:S(2)}) async-start(), calls=%async_computation.3 | async-start | bytes 8650752 | tf_op jit(solution)/shard_map/all_gather | solution.py:32
  9.0 326.0 %reduce-scatter.3.cloned.1.call-start = ((), (), s32[]{:S(2)}) async-start(), calls=%async_computation.4 | async-start | bytes 4718592 | tf_op jit(solution)/shard_map/reduce_scatter | solution.py:54
  146.7 22.2 %copy-start.1 = (f32[64,8,256]{2,1,0:T(8,128)S(1)}, f32[64,8,256]{2,1,0:T(8,128)}, u32[]{:S(2)}) copy-start(f32[64,8,256]{2,1,0:T(8,128)} %param.11) | copy-start | bytes 1572868
  146.8 22.1 %copy-start.4 = (f32[64,8,256]{2,1,0:T(8,128)S(1)}, f32[64,8,256]{2,1,0:T(8,128)}, u32[]{:S(2)}) copy-start(f32[64,8,256]{2,1,0:T(8,128)} %param.10) | copy-start | bytes 1572868
  146.8 22.1 %copy-start.5 = (f32[64,8,256]{2,1,0:T(8,128)S(1)}, f32[64,8,256]{2,1,0:T(8,128)}, u32[]{:S(2)}) copy-start(f32[64,8,256]{2,1,0:T(8,128)} %param.9) | copy-start | bytes 1572868
  146.8 22.1 %copy-start.6 = (f32[64,8,256]{2,1,0:T(8,128)S(1)}, f32[64,8,256]{2,1,0:T(8,128)}, u32[]{:S(2)}) copy-start(f32[64,8,256]{2,1,0:T(8,128)} %param.8) | copy-start | bytes 1572868
  147.6 2.6 collective-permute-start.1
  148.9 6.1 %collective-permute-start = (f32[1,8,256]{2,1,0:T(8,128)S(1)}, f32[1,8,256]{2,1,0:T(8,128)S(1)}, u32[]{:S(2)}, u32[]{:S(2)}) collective-permute-start(f32[1,8,256]{2,1,0:T(8,128)S(1)} %get-tuple-element.14), channel_id=1, source_target_pairs={{8,0},{16,8},{24,16},{32,24},{40,32},{48,40},{56,48},{64,56},{72,6... | collective-permute-start | bytes 24584 | tf_op jit(solution)/shard_map/ppermute | solution.py:22
  155.2 9.8 %collective-permute-start.2 = (f32[66,8,1]{2,1,0:T(8,128)S(1)}, f32[66,8,1]{2,1,0:T(8,128)S(1)}, u32[]{:S(2)}, u32[]{:S(2)}) collective-permute-start(f32[66,8,1]{2,1,0:T(8,128)S(1)} %get-tuple-element.11), channel_id=1, source_target_pairs={{1,0},{2,1},{3,2},{4,3},{5,4},{6,5},{7,6},{9,8},{10,9},{11,10},{12... | collective-permute-start | bytes 6344 | tf_op jit(solution)/shard_map/ppermute | solution.py:22
  158.8 10.1 %collective-permute-start.3 = (f32[66,8,1]{2,1,0:T(8,128)S(1)}, f32[66,8,1]{2,1,0:T(8,128)S(1)}, u32[]{:S(2)}, u32[]{:S(2)}) collective-permute-start(f32[66,8,1]{2,1,0:T(8,128)S(1)} %get-tuple-element.12), channel_id=1, source_target_pairs={{0,1},{1,2},{2,3},{3,4},{4,5},{5,6},{6,7},{8,9},{9,10},{10,11},{11... | collective-permute-start | bytes 6344 | tf_op jit(solution)/shard_map/ppermute | solution.py:21
  170.2 4.2 collective-permute-start.5
  173.1 4.9 collective-permute-start.4
  180.3 6.1 %collective-permute-start.6 = (f32[2,66,8,1]{1,2,3,0:T(8,128)S(1)}, f32[2,66,8,1]{1,2,3,0:T(8,128)S(1)}, u32[]{:S(2)}, u32[]{:S(2)}) collective-permute-start(f32[2,66,8,1]{1,2,3,0:T(8,128)S(1)} %copy.16), channel_id=1, source_target_pairs={{1,0},{2,1},{3,2},{4,3},{5,4},{6,5},{7,6},{9,8},{10,9},{11,10},{12... | collective-permute-start | bytes 12680 | tf_op jit(solution)/shard_map/ppermute | solution.py:22
  182.5 5.5 collective-permute-start.7
  193.2 141.8 %copy-start.2 = (bf16[64,2048]{1,0:T(8,128)(2,1)S(1)}, bf16[64,2048]{1,0:T(8,128)(2,1)}, u32[]{:S(2)}) copy-start(bf16[64,2048]{1,0:T(8,128)(2,1)} %param.12) | copy-start | bytes 786436
  193.2 357.1 %reduce-scatter.5.cloned.1.call-start = ((), (), s32[]{:S(2)}) async-start(), calls=%async_computation.5 | async-start | bytes 17301504 | tf_op jit(solution)/shard_map/reduce_scatter | solution.py:58
  362.0 188.3 %copy-start.3 = (bf16[64,8,256]{2,1,0:T(8,128)(2,1)S(1)}, bf16[64,8,256]{2,1,0:T(8,128)(2,1)}, u32[]{:S(2)}) copy-start(bf16[64,8,256]{2,1,0:T(8,128)(2,1)} %param.7) | copy-start | bytes 786436
Sparse Core Ops, SparseCore 0:
  10.5 72.3 all-gather.1
  193.3 141.6 reduce-scatter.2
  362.1 188.1 reduce-scatter.4
